TPU v7x, 32 devices: a whole 2x2x4 slice. The times are simulated.
32 devices in a mesh: grp: 2 (over y), tm: 4 (over z), row: 4 (over x, core).
Axes of the slice: x: 2, y: 2, z: 4, core: 2. Of those that a mesh axis runs over, the one named last changes fastest.
Arguments:
- frames: bfloat16 [16, 8, 24, 512], P(('grp', 'tm'), 'row'), parts along dimension 0, may hold values from -6 to 6
- w_in: bfloat16 [3, 3, 512, 512], P(None, None, None, ('tm', 'row')), may hold values from -0.046875 to 0.046875
- w_out: bfloat16 [3, 3, 512, 512], P(None, None, None, ('tm', 'row')), may hold values from -0.09375 to 0.09375
- decay_codes: int32 [512], replicated, may hold values from 0 to 15
- resets: int32 [16], P(('grp', 'tm')), parts along dimension 0, may hold values from 0 to 1, as said below
Outputs:
- mixed: bfloat16 [16, 8, 24, 512], P(('grp', 'tm'), 'row'), parts along dimension 0
There are 2 independent parts, one for each index of `grp`. A program takes and returns all parts, laid end to end along the dimension named above; an argument that names none is the same for every part. Nothing has to cross between parts.
Inputs may be any that keep to these rules, and one draw needn't show every extreme that they name: `decay_codes`: an entry of the table of 16 decays. `resets`: some frames start an episode and some do not.
All inputs are finite; a program needn't handle non-finite values.
Results may differ from a plain program's by a relative error of at most 0.005.
Values may be sent and summed in bfloat16 or wider, within the bound.
A program may use at most 64 MiB of HBM per device.

v0:
```python
import math

import jax
import jax.numpy as jnp
from jax import lax
from jax.sharding import PartitionSpec as P

LEVELS = 16
WINDOW = 4096


LOW_LOG = math.log(0.995)
HIGH_LOG = math.log(0.9999)


def entering(part, axis, combine, identity):
    place = lax.axis_index(axis)
    gathered = jax.tree.map(lambda a: lax.all_gather(a, axis), part)
    state = jax.tree.map(lambda a, e: jnp.zeros_like(a) + jnp.asarray(e, a.dtype), part, identity)

    def one(turn, state):
        return combine(
            state, jax.tree.map(lambda a: lax.dynamic_index_in_dim(a, turn, 0, False), gathered)
        )

    return lax.fori_loop(0, place, one, state)


def extended_2(array, sides, width):
    for axis, dim in sides:
        size, length = (lax.axis_size(axis), array.shape[dim])
        up = [(i, (i + 1) % size) for i in range(size - 1)]
        down = [(j, i) for i, j in up]
        last = lax.slice_in_dim(array, length - width, length, axis=dim)
        initial = lax.slice_in_dim(array, 0, width, axis=dim)
        before = lax.ppermute(last, axis, up)
        after = lax.ppermute(initial, axis, down)
        array = jnp.concatenate([before, array, after], axis=dim)
    return array


def frame_rates(decay_codes, frame_count):
    levels = jnp.arange(LEVELS, dtype=jnp.int32)
    log_table = LOW_LOG + levels.astype(jnp.float32) / (LEVELS - 1) * (HIGH_LOG - LOW_LOG)
    picked = (decay_codes[:, None] == levels[None, :]).astype(jnp.float32)
    log_rate = jnp.sum(picked * log_table[None, :], axis=1)
    return jnp.exp(WINDOW / frame_count * log_rate)


def conv_rows(rows, weight):
    count, height, width = (rows.shape[0], rows.shape[1] - 2, rows.shape[2])
    padded = jnp.pad(rows, ((0, 0), (0, 0), (1, 1), (0, 0)))
    total = jnp.zeros((count, height, width, weight.shape[3]), jnp.float32)
    for i in range(3):
        for j in range(3):
            total = total + jnp.einsum(
                "frwc,ck->frwk",
                padded[:, i : i + height, j : j + width],
                weight[i, j],
                preferred_element_type=jnp.float32,
            )
    return total


def carry_combine(earlier, later):
    return (earlier[0] * later[0], later[0][None, None, :] * earlier[1] + later[1])


def recurrence(drive, gates):

    def advance(carry, inputs):
        state, product = carry
        frame_drive, gate = inputs
        state = gate[None, None, :] * state + frame_drive
        product = product * gate
        return ((state, product), (state, product))

    start = (jnp.zeros(drive.shape[1:], jnp.float32), jnp.ones((drive.shape[3],), jnp.float32))
    (last_state, last_product), (states, products) = lax.scan(advance, start, (drive, gates))
    identity = (jnp.ones_like(last_product), jnp.zeros_like(last_state))
    before_product, before_state = entering(
        (last_product, last_state), "tm", carry_combine, identity
    )
    return states + products[:, None, None, :] * before_state[None]


def on_device(frames, w_in, w_out, decay_codes, resets):
    frame_count = frames.shape[0] * lax.axis_size("tm")
    rates = frame_rates(decay_codes, frame_count)
    gates = (1.0 - resets.astype(jnp.float32))[:, None] * rates[None, :]
    extended = extended_2(frames, (("row", 1),), 1)
    state = recurrence(
        conv_rows(extended, lax.all_gather(w_in, ("tm", "row"), axis=3, tiled=True)), gates
    )
    hidden = jax.nn.gelu(state).astype(jnp.bfloat16)
    hidden_rows = extended_2(hidden, (("row", 1),), 1)
    return conv_rows(hidden_rows, lax.all_gather(w_out, ("tm", "row"), axis=3, tiled=True)).astype(
        jnp.bfloat16
    )


def solution(mesh):
    return jax.shard_map(
        on_device,
        mesh=mesh,
        in_specs=(
            P(("grp", "tm"), "row", None, None),
            P(None, None, None, ("tm", "row")),
            P(None, None, None, ("tm", "row")),
            P(),
            P(("grp", "tm")),
        ),
        out_specs=P(("grp", "tm"), "row", None, None),
        check_vma=False,
    )
```

profile of v0, /device:TPU:1, one launch (start us, length us, event | category | flops | bytes accessed | tf_op | source)
XLA Modules:
  0.0 140.1 jit_solution(1108490326736602466)
XLA Ops:
  6.5 0.0 copy-start
  6.5 0.0 all-gather.6.cloned.1.call-start
  6.5 0.7 all-gather.6.cloned.1.call-update
  7.3 0.0 all-gather.8.cloned.1.call-start
  7.3 0.7 all-gather.8.cloned.1.call-update
  8.0 0.8 fusion.50
  8.8 4.5 %collective-permute-start = (bf16[2,1,24,512]{3,2,1,0:T(8,128)(2,1)S(1)}, bf16[2,1,24,512]{3,2,1,0:T(8,128)(2,1)S(1)}, u32[]{:S(2)}, u32[]{:S(2)}) collective-permute-start(bf16[2,1,24,512]{3,2,1,0:T(8,128)(2,1)S(1)} %get-tuple-element.146), channel_id=1, source_target_pairs={{0,1},{1,2},{2,3},{4,5},{5,6},{6,7},{8,9},{9,10},{10,11},{12,13},{... | collective-permute-start | bytes 147464 | tf_op jit(solution)/shard_map/ppermute | solution.py:36
  13.4 1.9 %collective-permute-start.1 = (bf16[2,1,24,512]{3,2,1,0:T(8,128)(2,1)S(1)}, bf16[2,1,24,512]{3,2,1,0:T(8,128)(2,1)S(1)}, u32[]{:S(2)}, u32[]{:S(2)}) collective-permute-start(bf16[2,1,24,512]{3,2,1,0:T(8,128)(2,1)S(1)} %get-tuple-element.147), channel_id=1, source_target_pairs={{1,0},{2,1},{3,2},{5,4},{6,5},{7,6},{9,8},{10,9},{11,10},{13,12},{... | collective-permute-start | bytes 147464 | tf_op jit(solution)/shard_map/ppermute | solution.py:37
  15.3 0.8 select_reduce_fusion
  16.1 0.7 convert_subtract_fusion
  16.7 0.1 broadcast_multiply_fusion
  16.8 0.0 collective-permute-done
  16.8 2.0 %collective-permute-done.1 = bf16[2,1,24,512]{3,2,1,0:T(8,128)(2,1)S(1)} collective-permute-done((bf16[2,1,24,512]{3,2,1,0:T(8,128)(2,1)S(1)}, bf16[2,1,24,512]{3,2,1,0:T(8,128)(2,1)S(1)}, u32[]{:S(2)}, u32[]{:S(2)}) %collective-permute-start.1) | collective-permute-done | bytes 49184 | tf_op jit(solution)/shard_map/ppermute | solution.py:37
  18.8 1.0 fusion.12
  19.7 45.6 %all-gather.6.cloned.1.call-done = bf16[3,3,512,512]{2,3,1,0:T(8,128)(2,1)} async-done(((bf16[3,3,512,32]{2,3,1,0:T(8,128)(2,1)}), bf16[3,3,512,512]{2,3,1,0:T(8,128)(2,1)}) %all-gather.6.cloned.1.call-update) | async-done | bytes 4718608 | tf_op jit(solution)/shard_map/all_gather | solution.py:93
  65.3 1.4 fusion.6
  66.7 1.3 fusion.5
  68.0 1.3 convolution_add_fusion.13
  69.4 1.3 convolution_add_fusion.12
  70.7 1.3 convolution_add_fusion.11
  72.1 0.0 copy-done
  72.1 1.3 convolution_add_fusion.10
  73.4 1.4 convolution_add_fusion.9
  74.8 1.3 convolution_add_fusion.8
  76.1 1.3 fusion.1
  77.5 0.3 while.30
  77.7 9.7 %all-gather.2 = f32[4,1,512]{2,1,0:T(1,128)S(1)} all-gather(f32[1,1,512]{2,1,0:T(1,128)S(1)} %bitcast.175), channel_id=2, replica_groups=mesh['grp'=2,'tm'=4,'row'=4] {'tm'}, dimensions={0}, use_global_device_ids=true | all-gather | bytes 10240 | tf_op jit(solution)/shard_map/all_gather | solution.py:18
  87.5 14.0 %all-gather.1 = f32[8,24,512]{2,1,0:T(8,128)S(1)} all-gather(f32[2,24,512]{2,1,0:T(8,128)S(1)} %get-tuple-element.92), channel_id=3, replica_groups=mesh['grp'=2,'tm'=4,'row'=4] {'tm'}, dimensions={0}, use_global_device_ids=true | all-gather | bytes 491520 | tf_op jit(solution)/shard_map/all_gather | solution.py:18
  101.5 0.1 fusion.20
  101.6 7.5 %collective-permute-start.2 = (bf16[2,1,24,512]{3,2,1,0:T(8,128)(2,1)S(1)}, bf16[2,1,24,512]{3,2,1,0:T(8,128)(2,1)S(1)}, u32[]{:S(2)}, u32[]{:S(2)}) collective-permute-start(bf16[2,1,24,512]{3,2,1,0:T(8,128)(2,1)S(1)} %get-tuple-element.144), channel_id=1, source_target_pairs={{0,1},{1,2},{2,3},{4,5},{5,6},{6,7},{8,9},{9,10},{10,11},{12,13},{... | collective-permute-start | bytes 147464 | tf_op jit(solution)/shard_map/ppermute | solution.py:36
  109.1 1.9 %collective-permute-start.3 = (bf16[2,1,24,512]{3,2,1,0:T(8,128)(2,1)S(1)}, bf16[2,1,24,512]{3,2,1,0:T(8,128)(2,1)S(1)}, u32[]{:S(2)}, u32[]{:S(2)}) collective-permute-start(bf16[2,1,24,512]{3,2,1,0:T(8,128)(2,1)S(1)} %get-tuple-element.145), channel_id=1, source_target_pairs={{1,0},{2,1},{3,2},{5,4},{6,5},{7,6},{9,8},{10,9},{11,10},{13,12},{... | collective-permute-start | bytes 147464 | tf_op jit(solution)/shard_map/ppermute | solution.py:37
  111.1 9.4 %all-gather.8.cloned.1.call-done = bf16[3,3,512,512]{2,3,1,0:T(8,128)(2,1)} async-done(((bf16[3,3,512,32]{2,3,1,0:T(8,128)(2,1)}), bf16[3,3,512,512]{2,3,1,0:T(8,128)(2,1)}) %all-gather.8.cloned.1.call-update) | async-done | bytes 4718608 | tf_op jit(solution)/shard_map/all_gather | solution.py:97
  120.4 0.0 collective-permute-done.2
  120.4 1.3 fusion.4
  121.8 0.0 collective-permute-done.3
  121.8 0.1 select_maximum_fusion
  121.9 1.3 fusion.3
  123.2 1.3 convolution_add_fusion.7
  124.6 1.3 convolution_add_fusion.6
  125.9 1.3 convolution_add_fusion.5
  127.2 1.3 convolution_add_fusion.4
  128.6 1.3 convolution_add_fusion.3
  129.9 1.3 convolution_add_fusion.2
  131.3 2.0 %fusion.2 = bf16[2,2,24,512]{3,2,1,0:T(8,128)(2,1)} fusion(f32[2,2,24,512]{3,2,1,0:T(8,128)S(1)} %fusion.3, f32[2,2,24,512]{3,2,1,0:T(8,128)S(1)} %convolution_add_fusion.2, bf16[3,3,512,512]{2,3,1,0:T(8,128)(2,1)} %all-gather.8.cloned.1.call-done, bf16[2,1,24,512]{3,2,1,0:T(8,128)(2,1)S(1)} %collective-permute-done.3, bf16[2,2,24,512]{3,2,1,0:T(8,128)(2,1)S(1)} %fusion.20), kind=kOutput, calls=%fused_computation.23 | convolution fusion | flops 50774016 | bytes 1163264 | tf_op jit(solution)/shard_map/frwc,ck->frwk/dot_general | solution.py:56
  (18 shorter events, 0.2 us)
Async XLA Ops:
  6.5 65.5 %copy-start = (bf16[2,2,24,512]{3,2,1,0:T(8,128)(2,1)S(1)}, bf16[2,2,24,512]{3,2,1,0:T(8,128)(2,1)}, u32[]{:S(2)}) copy-start(bf16[2,2,24,512]{3,2,1,0:T(8,128)(2,1)} %param.9) | copy-start | bytes 294916
  6.5 58.8 %all-gather.6.cloned.1.call-start = ((), (), s32[]{:S(2)}) async-start(), calls=%async_computation | async-start | bytes 5013504 | tf_op jit(solution)/shard_map/all_gather | solution.py:93
  7.3 113.2 %all-gather.8.cloned.1.call-start = ((), (), s32[]{:S(2)}) async-start(), calls=%async_computation.1 | async-start | bytes 5013504 | tf_op jit(solution)/shard_map/all_gather | solution.py:97
  8.8 8.0 %collective-permute-start = (bf16[2,1,24,512]{3,2,1,0:T(8,128)(2,1)S(1)}, bf16[2,1,24,512]{3,2,1,0:T(8,128)(2,1)S(1)}, u32[]{:S(2)}, u32[]{:S(2)}) collective-permute-start(bf16[2,1,24,512]{3,2,1,0:T(8,128)(2,1)S(1)} %get-tuple-element.146), channel_id=1, source_target_pairs={{0,1},{1,2},{2,3},{4,5},{5,6},{6,7},{8,9},{9,10},{10,11},{12,13},{... | collective-permute-start | bytes 147464 | tf_op jit(solution)/shard_map/ppermute | solution.py:36
  13.4 5.4 %collective-permute-start.1 = (bf16[2,1,24,512]{3,2,1,0:T(8,128)(2,1)S(1)}, bf16[2,1,24,512]{3,2,1,0:T(8,128)(2,1)S(1)}, u32[]{:S(2)}, u32[]{:S(2)}) collective-permute-start(bf16[2,1,24,512]{3,2,1,0:T(8,128)(2,1)S(1)} %get-tuple-element.147), channel_id=1, source_target_pairs={{1,0},{2,1},{3,2},{5,4},{6,5},{7,6},{9,8},{10,9},{11,10},{13,12},{... | collective-permute-start | bytes 147464 | tf_op jit(solution)/shard_map/ppermute | solution.py:37
  101.6 18.8 %collective-permute-start.2 = (bf16[2,1,24,512]{3,2,1,0:T(8,128)(2,1)S(1)}, bf16[2,1,24,512]{3,2,1,0:T(8,128)(2,1)S(1)}, u32[]{:S(2)}, u32[]{:S(2)}) collective-permute-start(bf16[2,1,24,512]{3,2,1,0:T(8,128)(2,1)S(1)} %get-tuple-element.144), channel_id=1, source_target_pairs={{0,1},{1,2},{2,3},{4,5},{5,6},{6,7},{8,9},{9,10},{10,11},{12,13},{... | collective-permute-start | bytes 147464 | tf_op jit(solution)/shard_map/ppermute | solution.py:36
  109.1 12.6 %collective-permute-start.3 = (bf16[2,1,24,512]{3,2,1,0:T(8,128)(2,1)S(1)}, bf16[2,1,24,512]{3,2,1,0:T(8,128)(2,1)S(1)}, u32[]{:S(2)}, u32[]{:S(2)}) collective-permute-start(bf16[2,1,24,512]{3,2,1,0:T(8,128)(2,1)S(1)} %get-tuple-element.145), channel_id=1, source_target_pairs={{1,0},{2,1},{3,2},{5,4},{6,5},{7,6},{9,8},{10,9},{11,10},{13,12},{... | collective-permute-start | bytes 147464 | tf_op jit(solution)/shard_map/ppermute | solution.py:37
Sparse Core Ops, SparseCore 0:
  9.5 55.7 all-gather.5
  67.5 52.8 all-gather.7
where the time goes:
time: 141 us; the launch traced here: 140 us
  waiting for transfers between devices  58.3 us (41%)
  matrix products  24.8 us (18%)
  blocking collectives  23.8 us (17%)
  starting transfers between devices  15.9 us (11%)
  between operations  13.6 us (10%)
  other arithmetic  2.77 us (2%)
    all_gather x1, waiting for transfers between devices, on_device(): lax.all_gather(w_in, ('tm', 'row'), axis=3, tiled=True)  45.6 us
    dot_general x18, matrix products, conv_rows(): jnp.einsum('frwc,ck->frwk', padded[:, i:i + height, j:j + width], weight[...  24.8 us
    all_gather x2, blocking collectives, entering(): gathered = jax.tree.map(lambda a: lax.all_gather(a, axis), part)  23.8 us
    ppermute x2, starting transfers between devices, extended_2(): before = lax.ppermute(last, axis, up)  12 us
    all_gather x1, waiting for transfers between devices, on_device(): lax.all_gather(w_out, ('tm', 'row'), axis=3, tiled=True)  9.38 us
    ppermute x2, starting transfers between devices, extended_2(): after = lax.ppermute(initial, axis, down)  3.84 us
  transfers between devices with their start and end apart: 6, of which 3 were waited for; matrix products, arithmetic and copies ran while one was open for 12% of the time, Pallas kernels for 0%

commit v1 on v0

--- a/solution.py
+++ b/solution.py
@@ -84,7 +84,7 @@
     return states + products[:, None, None, :] * before_state[None]
 
 
-def on_device(frames, w_in, w_out, decay_codes, resets):
+def by_filters(frames, w_in, w_out, decay_codes, resets):
     frame_count = frames.shape[0] * lax.axis_size("tm")
     rates = frame_rates(decay_codes, frame_count)
     gates = (1.0 - resets.astype(jnp.float32))[:, None] * rates[None, :]
@@ -97,6 +97,64 @@
     return conv_rows(hidden_rows, lax.all_gather(w_out, ("tm", "row"), axis=3, tiled=True)).astype(
         jnp.bfloat16
     )
+
+
+def taps_matrix(weight):
+    depth, width = weight.shape[2], weight.shape[3]
+    return jnp.transpose(weight, (2, 0, 1, 3)).reshape(depth, 9 * width)
+
+
+def conv_all(rows, weight):
+    frames, height, width, depth = rows.shape
+    out = weight.shape[3]
+    taps = jnp.dot(
+        rows.reshape(-1, depth), taps_matrix(weight), preferred_element_type=jnp.float32
+    ).reshape(frames, height, width, 9 * out)
+    padded = jnp.pad(taps, ((0, 0), (1, 1), (1, 1), (0, 0)))
+    total = jnp.zeros((frames, height, width, out), jnp.float32)
+    for i in range(3):
+        for j in range(3):
+            at = (3 * i + j) * out
+            total = total + padded[:, i : i + height, j : j + width, at : at + out]
+    return total
+
+
+def by_activations(frames, w_in, w_out, decay_codes, resets):
+    axes = ("tm", "row")
+    tm, row = (lax.axis_size("tm"), lax.axis_size("row"))
+    own, height, width, depth = frames.shape
+    out = w_in.shape[3]
+    count = own * tm
+    place = lax.axis_index("tm") * row + lax.axis_index("row")
+    codes = lax.dynamic_slice_in_dim(decay_codes, place * out, out)
+    rates = frame_rates(codes, count)
+    all_resets = lax.all_gather(resets.reshape(1, own), "tm", axis=0, tiled=True).reshape(count)
+    gates = (1.0 - all_resets.astype(jnp.float32))[:, None] * rates[None, :]
+    blocks = lax.all_gather(frames, axes, axis=0, tiled=False)
+    blocks = blocks.reshape(tm, row, own, height, width, depth)
+    everything = jnp.transpose(blocks, (0, 2, 1, 3, 4, 5)).reshape(
+        count, row * height, width, depth
+    )
+    drive = conv_all(everything, w_in)
+    state = jnp.zeros(drive.shape[1:], jnp.float32)
+    hidden = []
+    for t in range(count):
+        state = gates[t][None, None, :] * state + drive[t]
+        hidden.append(jax.nn.gelu(state).astype(jnp.bfloat16))
+    hidden = lax.all_gather(jnp.stack(hidden), axes, axis=0, tiled=False)
+    hidden = jnp.transpose(hidden, (1, 2, 3, 0, 4)).reshape(count, row * height, width, -1)
+    mixed = conv_all(hidden, w_out).astype(jnp.bfloat16)
+    parts = jnp.transpose(
+        mixed.reshape(tm, own, row, height, width, out), (0, 2, 1, 3, 4, 5)
+    ).reshape(tm * row, own, height, width, out)
+    swapped = lax.all_to_all(parts, axes, 0, 0, tiled=True)
+    return jnp.transpose(swapped, (1, 2, 3, 0, 4)).reshape(own, height, width, -1)
+
+
+def on_device(frames, w_in, w_out, decay_codes, resets):
+    devices = lax.axis_size("tm") * lax.axis_size("row")
+    plan = by_activations if frames.size * devices < w_in.size * devices else by_filters
+    return plan(frames, w_in, w_out, decay_codes, resets)
 
 
 def solution(mesh):

time: 141 us -> 161 us (1.14)
  waiting for transfers between devices: 58.3 us -> 95.2 us
  local copies, waits for them, and re-layouts: 0.97 us -> 28 us
  matrix products: 24.8 us -> 2.05 us
  starting transfers between devices: 15.9 us -> 0.04 us
  blocking collectives: 23.8 us -> 17 us
    all_gather x2, waiting for transfers between devices: 55 us -> 94.5 us  [the longest x1 60.9 us: by_activations(): hidden = lax.all_gather(jnp.stack(hidden), axes, axis=0, tiled=False)]
    all_gather x2 -> x0, blocking collectives: 23.8 us -> none  [entering(): gathered = jax.tree.map(lambda a: lax.all_gather(a, axis), part)]
    dot_general x18 -> x2, matrix products: 24.8 us -> 2.05 us  [conv_all(): jnp.dot(rows.reshape(-1, depth), taps_matrix(weight), preferred_element_t...]
    ppermute x4 -> x0, starting transfers between devices: 15.8 us -> none  [the longest x2 12 us: extended_2(): before = lax.ppermute(last, axis, up)]
    all_gather x0 -> x1, local copies, waits for them, and re-layouts: none -> 12.8 us  [by_activations(): hidden = lax.all_gather(jnp.stack(hidden), axes, axis=0, tiled=False)]
    all_to_all x0 -> x1, blocking collectives: none -> 9.73 us  [by_activations(): swapped = lax.all_to_all(parts, axes, 0, 0, tiled=True)]
    dot_general x0 -> x1, local copies, waits for them, and re-layouts: none -> 8.42 us  [conv_all(): jnp.dot(rows.reshape(-1, depth), taps_matrix(weight), preferred_element_t...]
    unnamed x0 -> x1, blocking collectives: none -> 7.25 us
  transfers between devices with their start and end apart: 6 -> 2, of which waited for: 3 -> 2; matrix products, arithmetic and copies ran while one was open for 12% -> 2% of each run, Pallas kernels for 0% -> 0%
where the time goes in v1:
time: 161 us; the launch traced here: 160 us
  waiting for transfers between devices  95.2 us (59%)
  local copies, waits for them, and re-layouts  28 us (17%)
  blocking collectives  17 us (11%)
  between operations  14.2 us (9%)
  other arithmetic  3.09 us (2%)
  matrix products  2.05 us (1%)
    all_gather x1, waiting for transfers between devices, by_activations(): hidden = lax.all_gather(jnp.stack(hidden), axes, axis=0, tiled=False)  60.9 us
    all_gather x1, waiting for transfers between devices, by_activations(): blocks = lax.all_gather(frames, axes, axis=0, tiled=False)  33.6 us
    all_gather x1, local copies, waits for them, and re-layouts, by_activations(): hidden = lax.all_gather(jnp.stack(hidden), axes, axis=0, tiled=False)  12.8 us
    all_to_all x1, blocking collectives, by_activations(): swapped = lax.all_to_all(parts, axes, 0, 0, tiled=True)  9.73 us
    dot_general x1, local copies, waits for them, and re-layouts, conv_all(): jnp.dot(rows.reshape(-1, depth), taps_matrix(weight), preferred_element_t...  8.42 us
    unnamed x1, blocking collectives  7.25 us
    unnamed x11, local copies, waits for them, and re-layouts  3.39 us
  transfers between devices with their start and end apart: 2, of which 2 were waited for; matrix products, arithmetic and copies ran while one was open for 2% of the time, Pallas kernels for 0%

profile of v1, /device:TPU:1, one launch (start us, length us, event | category | flops | bytes accessed | tf_op | source)
XLA Modules:
  0.0 159.5 jit_solution(18434706689439194062)
XLA Ops:
  6.5 0.0 copy-start
  6.5 0.0 all-gather.6.cloned.1.call-start
  6.5 0.7 all-gather.6.cloned.1.call-update
  7.3 0.0 all-gather.8.cloned.1.call-start
  7.3 1.2 dynamic-slice
  9.2 0.9 dynamic-update-slice
  10.1 7.3 %all-reduce.2 = s32[8]{0:T(128)S(1)} all-reduce(s32[8]{0:T(128)S(1)} %dynamic-update-slice), channel_id=2, replica_groups=mesh['grp'=2,'tm'=4,'row'=4] {'tm'}, use_global_device_ids=true, to_apply=%add.2 | all-reduce | flops 8 | bytes 64
  17.3 0.8 dynamic_slice.3
  18.1 0.1 select_reduce_fusion
  18.2 0.1 broadcast_multiply_fusion
  18.3 33.6 %all-gather.6.cloned.1.call-done = bf16[32,2,24,512]{3,2,1,0:T(8,128)(2,1)} async-done(((bf16[2,2,24,512]{3,2,1,0:T(8,128)(2,1)}), bf16[32,2,24,512]{3,2,1,0:T(8,128)(2,1)}) %all-gather.6.cloned.1.call-update) | async-done | bytes 1572880 | tf_op jit(solution)/shard_map/all_gather | solution.py:133
  51.9 1.5 copy.19
  53.4 0.0 copy-done
  53.4 1.0 fusion.89
  54.4 1.2 fusion.7
  55.6 0.1 fusion.87
  55.7 0.1 fusion.86
  55.8 0.1 fusion.85
  55.9 0.1 fusion.84
  55.9 0.1 fusion.83
  56.0 0.1 fusion.82
  56.1 0.1 fusion.81
  56.1 0.0 copy-start.1
  56.1 0.7 copy-done.1
  56.9 0.0 all-gather.8.cloned.1.call-update
  56.9 60.9 %all-gather.8.cloned.1.call-done = bf16[128,8,24,32]{3,2,1,0:T(8,128)(2,1)} async-done(((bf16[8,8,24,32]{3,2,1,0:T(8,128)(2,1)}), bf16[128,8,24,32]{3,2,1,0:T(8,128)(2,1)}) %all-gather.8.cloned.1.call-update) | async-done | bytes 1572880 | tf_op jit(solution)/shard_map/all_gather | solution.py:144
  117.8 12.8 %copy.26 = bf16[16,8,8,24,32]{4,0,3,2,1:T(8,128)(2,1)} copy(bf16[16,8,8,24,32]{4,3,2,1,0:T(8,128)(2,1)} %bitcast.54) | data formatting | bytes 3145728 | tf_op jit(solution)/shard_map/all_gather | solution.py:144
  130.6 0.0 copy-start.2
  130.6 8.4 %dot_general.12 = bf16[8,8,24,512]{3,2,1,0:T(8,128)(2,1)S(1)} reshape(bf16[8,8,24,16,32]{4,3,2,1,0:T(8,128)(2,1)} %bitcast.53) | data formatting | bytes 3145728 | tf_op jit(solution)/shard_map/dot_general | solution.py:110
  139.0 0.0 copy-done.2
  139.0 1.0 fusion.90
  140.1 1.2 fusion.16
  141.3 0.3 reshape.80
  141.6 9.7 %all_to_all.5 = bf16[16,2,1536]{2,1,0:T(2,128)(2,1)S(1)} all-to-all(bf16[16,2,1536]{2,1,0:T(2,128)(2,1)S(1)} %reshape.80), channel_id=1, replica_groups=mesh['grp'=2,'tm'=4,'row'=4] {'tm','row'}, dimensions={0} | all-to-all | bytes 196608 | tf_op jit(solution)/shard_map/all_to_all | solution.py:150
  151.3 0.2 reshape.81
  151.6 0.2 copy.22
  151.7 1.0 reshape.64
  (7 shorter events, 0.1 us)
Async XLA Ops:
  6.5 46.8 %copy-start = (bf16[3,3,512,32]{2,3,1,0:T(8,128)(2,1)S(1)}, bf16[3,3,512,32]{2,3,1,0:T(8,128)(2,1)}, u32[]{:S(2)}) copy-start(bf16[3,3,512,32]{2,3,1,0:T(8,128)(2,1)} %param.6) | copy-start | bytes 884740
  6.5 45.3 %all-gather.6.cloned.1.call-start = ((), (), s32[]{:S(2)}) async-start(), calls=%async_computation.1 | async-start | bytes 1671168 | tf_op jit(solution)/shard_map/all_gather | solution.py:133
  7.3 110.6 %all-gather.8.cloned.1.call-start = ((), (), s32[]{:S(2)}) async-start(), calls=%async_computation.2 | async-start | bytes 6684672 | tf_op jit(solution)/shard_map/all_gather | solution.py:144
  56.1 0.7 copy-start.1
  130.6 8.4 %copy-start.2 = (bf16[3,3,512,32]{2,3,1,0:T(8,128)(2,1)S(1)}, bf16[3,3,512,32]{2,3,1,0:T(8,128)(2,1)}, u32[]{:S(2)}) copy-start(bf16[3,3,512,32]{2,3,1,0:T(8,128)(2,1)} %param.7) | copy-start | bytes 884740
Sparse Core Ops, SparseCore 0:
  9.6 42.1 all-gather.5
  57.0 60.7 all-gather.7

commit v2 on v0

--- a/solution.py
+++ b/solution.py
@@ -1,8 +1,11 @@
+import functools
 import math
 
 import jax
 import jax.numpy as jnp
 from jax import lax
+from jax.experimental import pallas as pl
+from jax.experimental.pallas import tpu as pltpu
 from jax.sharding import PartitionSpec as P
 
 LEVELS = 16
@@ -84,7 +87,7 @@
     return states + products[:, None, None, :] * before_state[None]
 
 
-def on_device(frames, w_in, w_out, decay_codes, resets):
+def by_filters(frames, w_in, w_out, decay_codes, resets):
     frame_count = frames.shape[0] * lax.axis_size("tm")
     rates = frame_rates(decay_codes, frame_count)
     gates = (1.0 - resets.astype(jnp.float32))[:, None] * rates[None, :]
@@ -97,6 +100,360 @@
     return conv_rows(hidden_rows, lax.all_gather(w_out, ("tm", "row"), axis=3, tiled=True)).astype(
         jnp.bfloat16
     )
+
+
+MESH = pl.DeviceIdType.MESH
+WIDE = 32
+LANES = 128
+
+
+def layer_kernel(
+    tm,
+    width,
+    frames_ref,
+    win_ref,
+    wout_ref,
+    codes_ref,
+    resets_ref,
+    out_ref,
+    blocks,
+    image,
+    hidden_own,
+    hidden_in,
+    hidden,
+    banks,
+    keep,
+    result_out,
+    result_in,
+    f_send,
+    f_recv,
+    k_send,
+    k_recv,
+    w_send,
+    w_recv,
+    e_send,
+    e_recv,
+    h_send,
+    h_recv,
+    o_send,
+    o_recv,
+    own_sem,
+):
+    z, r = (lax.axis_index("tm"), lax.axis_index("row"))
+    rows = lax.axis_size("row")
+    sibling = r + 1 - 2 * lax.rem(r, 2)
+    partner = lax.rem(r + 2, 4)
+    shard = win_ref.shape[2]
+    own = frames_ref.shape[0] // (2 * width)
+    count = own * tm
+    depth = frames_ref.shape[1]
+    started = []
+    mine_copies = []
+
+    def remote(src, dst, send, recv, **where):
+        return pltpu.make_async_remote_copy(
+            src_ref=src, dst_ref=dst, send_sem=send, recv_sem=recv,
+            device_id=where, device_id_type=MESH,
+        )
+
+    barrier = pltpu.get_barrier_semaphore()
+    for d in range(1, tm):
+        pl.semaphore_signal(
+            barrier, inc=1, device_id={"tm": lax.rem(z + d, tm)}, device_id_type=MESH
+        )
+    for d in range(1, rows):
+        pl.semaphore_signal(
+            barrier, inc=1, device_id={"row": lax.rem(r + d, rows)}, device_id_type=MESH
+        )
+
+    for f in range(own):
+        keep[z, pl.ds(f, 1), :] = jnp.full(
+            (1, LANES), 1.0 - resets_ref[f].astype(jnp.float32), jnp.float32
+        )
+    pl.semaphore_wait(barrier, tm + rows - 2)
+
+    def bank_slot(b, i, place):
+        return banks.at[b, i, :, pl.ds(pl.multiple_of(place * shard, shard), shard), :]
+
+    def bank_sends(b, ref):
+        copies = []
+        for i in range(3):
+            for kind, to in ((0, partner), (1, sibling)):
+                copy = remote(
+                    ref.at[i], bank_slot(b, i, r), w_send.at[b, kind, i], w_recv.at[b, kind, i],
+                    row=to,
+                )
+                copy.start()
+                copies.append(copy)
+            mine = pltpu.make_async_copy(ref.at[i], bank_slot(b, i, r), own_sem.at[b, i])
+            mine.start()
+            mine_copies.append(mine)
+        started.extend(c.wait_send for c in copies)
+        return copies
+
+    def bank_relay(b, i, copies):
+        copies[2 * i].wait_recv()
+        slot = bank_slot(b, i, partner)
+        copy = remote(slot, slot, w_send.at[b, 2, i], w_recv.at[b, 2, i], row=sibling)
+        copy.start()
+        started.append(copy.wait_send)
+        return copy
+
+    def spread(make):
+        copies = []
+        for d in (1, tm - 1) + tuple(range(2, tm - 1)):
+            copy = make(d, lax.rem(z + d, tm))
+            copy.start()
+            started.append(copy.wait_send)
+            copies.append((d, copy))
+        return copies
+
+    def edge_copies(stage, array, d, part):
+        slot = d + stage * tm
+        up = remote(
+            part(array, 1), part(array, 3), e_send.at[0, slot], e_recv.at[0, slot],
+            row=jnp.maximum(r - 1, 0),
+        )
+        down = remote(
+            part(array, 2), part(array, 0), e_send.at[1, slot], e_recv.at[1, slot],
+            row=jnp.minimum(r + 1, rows - 1),
+        )
+        return (up, down)
+
+    def start_edges(pair):
+        @pl.when(r > 0)
+        def _():
+            pair[0].start()
+
+        @pl.when(r < rows - 1)
+        def _():
+            pair[1].start()
+
+    def wait_edges(pairs):
+        @pl.when(r > 0)
+        def _():
+            for up, down in pairs:
+                down.wait_recv()
+
+        @pl.when(r < rows - 1)
+        def _():
+            for up, down in pairs:
+                up.wait_recv()
+
+    def finish_edges(pairs):
+        @pl.when(r > 0)
+        def _():
+            for up, down in pairs:
+                up.wait_send()
+
+        @pl.when(r < rows - 1)
+        def _():
+            for up, down in pairs:
+                down.wait_send()
+
+    keeps = spread(
+        lambda d, to: remote(keep.at[z], keep.at[z], k_send.at[d], k_recv.at[d], tm=to)
+    )
+    arriving = spread(
+        lambda d, to: remote(frames_ref, blocks.at[z], f_send.at[d], f_recv.at[d], tm=to)
+    )
+    in_copies = bank_sends(0, win_ref)
+
+    @pl.when(r == 0)
+    def _():
+        image[0] = jnp.zeros(image.shape[1:], image.dtype)
+        hidden[0] = jnp.zeros(hidden.shape[1:], hidden.dtype)
+
+    @pl.when(r == rows - 1)
+    def _():
+        image[3] = jnp.zeros(image.shape[1:], image.dtype)
+        hidden[3] = jnp.zeros(hidden.shape[1:], hidden.dtype)
+
+    gap = jnp.zeros((WIDE - width, depth), jnp.bfloat16)
+
+    def place_frames(block, source):
+        for f in range(own):
+            for y in range(2):
+                at = (2 * f + y) * width
+                image[1 + y, source * own + f] = jnp.concatenate(
+                    [block[at : at + width, :], gap], axis=0
+                )
+
+    def frame_part(source):
+        return lambda array, y: array.at[y, pl.ds(source * own, own)]
+
+    place_frames(frames_ref, z)
+    edges = [edge_copies(0, image, 0, frame_part(z))]
+    start_edges(edges[0])
+    relays = []
+    for n, (d, copy) in enumerate(arriving):
+        copy.wait_recv()
+        source = lax.rem(z - d + tm, tm)
+        place_frames(blocks.at[source], source)
+        pair = edge_copies(0, image, d, frame_part(source))
+        start_edges(pair)
+        edges.append(pair)
+        if n < 3:
+            relays.append(bank_relay(0, n, in_copies))
+    for n in range(len(relays), 3):
+        relays.append(bank_relay(0, n, in_copies))
+    out_copies = bank_sends(1, wout_ref)
+    for _, copy in keeps:
+        copy.wait_recv()
+    for n in range(3):
+        in_copies[2 * n + 1].wait_recv()
+        relays[n].wait_recv()
+        mine_copies[n].wait()
+    wait_edges(edges)
+
+    def conv(array, b):
+        total = None
+        for i in range(3):
+            term = lax.dot_general(
+                array[i : i + 2].reshape(2 * count * WIDE, depth),
+                banks[b, i].reshape(3 * LANES, depth),
+                (((1,), (1,)), ((), ())),
+                preferred_element_type=jnp.float32,
+            )
+            total = term if total is None else total + term
+        size = 2 * count * WIDE
+        left = pltpu.roll(total[:, :LANES], 1, 0)
+        right = pltpu.roll(total[:, 2 * LANES :], size - 1, 0)
+        return (left + total[:, LANES : 2 * LANES] + right).reshape(2, count, WIDE, LANES)
+
+    drive = conv(image, 0)
+    codes = codes_ref[:, pl.ds(pl.multiple_of(z * LANES, LANES), LANES)].astype(jnp.float32)
+    rates = jnp.exp(
+        WINDOW / count * (LOW_LOG + codes / (LEVELS - 1) * (HIGH_LOG - LOW_LOG))
+    )
+    state = jnp.zeros((2, width, LANES), jnp.float32)
+    tail = jnp.zeros((2, WIDE - width, LANES), jnp.bfloat16)
+    here = pl.ds(pl.multiple_of(z * LANES, LANES), LANES)
+    for t in range(count):
+        gate = keep[t // own, t % own : t % own + 1, :] * rates
+        state = gate[None] * state + drive[:, t, :width]
+        value = jax.nn.gelu(state).astype(jnp.bfloat16)
+        hidden_own[t] = value.reshape(2 * width, LANES)
+        hidden[1:3, t, :, here] = jnp.concatenate([value, tail], axis=1)
+
+    arriving = spread(
+        lambda d, to: remote(hidden_own, hidden_in.at[z], h_send.at[d], h_recv.at[d], tm=to)
+    )
+
+    def lane_part(source):
+        lanes = pl.ds(pl.multiple_of(source * LANES, LANES), LANES)
+        return lambda array, y: array.at[y, :, :, lanes]
+
+    second = [edge_copies(1, hidden, 0, lane_part(z))]
+    start_edges(second[0])
+    relays = []
+    for n, (d, copy) in enumerate(arriving):
+        if n < 3:
+            relays.append(bank_relay(1, n, out_copies))
+        copy.wait_recv()
+        source = lax.rem(z - d + tm, tm)
+        lanes = pl.ds(pl.multiple_of(source * LANES, LANES), LANES)
+        for t in range(count):
+            value = hidden_in[source, t].reshape(2, width, LANES)
+            hidden[1:3, t, :, lanes] = jnp.concatenate([value, tail], axis=1)
+        pair = edge_copies(1, hidden, d, lane_part(source))
+        start_edges(pair)
+        second.append(pair)
+    for n in range(len(relays), 3):
+        relays.append(bank_relay(1, n, out_copies))
+    for n in range(3):
+        out_copies[2 * n + 1].wait_recv()
+        relays[n].wait_recv()
+    wait_edges(second)
+    for n in range(3, 6):
+        mine_copies[n].wait()
+    mixed = conv(hidden, 1).astype(jnp.bfloat16)
+    for k in range(tm):
+        result_out[k] = jnp.concatenate(
+            [mixed[y, k * own + f, :width] for f in range(own) for y in range(2)], axis=0
+        )
+    leaving = spread(
+        lambda d, to: remote(
+            result_out.at[to], result_in.at[z], o_send.at[d], o_recv.at[d], tm=to
+        )
+    )
+    out_ref[:, here] = result_out[z]
+    for d, copy in leaving:
+        copy.wait_recv()
+        source = lax.rem(z - d + tm, tm)
+        out_ref[:, pl.ds(pl.multiple_of(source * LANES, LANES), LANES)] = result_in[source]
+    for wait in started:
+        wait()
+    finish_edges(edges)
+    finish_edges(second)
+
+
+def by_channels(frames, w_in, w_out, decay_codes, resets):
+    tm = lax.axis_size("tm")
+    own, height, width, depth = frames.shape
+    shard = w_in.shape[3]
+    count = own * tm
+    flat = own * height * width
+    dma = pltpu.SemaphoreType.DMA
+    vmem = pl.BlockSpec(memory_space=pltpu.VMEM)
+    out = pl.pallas_call(
+        functools.partial(layer_kernel, tm, width),
+        out_shape=jax.ShapeDtypeStruct((flat, depth), jnp.bfloat16),
+        in_specs=[vmem] * 4 + [pl.BlockSpec(memory_space=pltpu.SMEM)],
+        out_specs=vmem,
+        scratch_shapes=[
+            pltpu.VMEM((tm, flat, depth), jnp.bfloat16),
+            pltpu.VMEM((4, count, WIDE, depth), jnp.bfloat16),
+            pltpu.VMEM((count, 2 * width, LANES), jnp.bfloat16),
+            pltpu.VMEM((tm, count, 2 * width, LANES), jnp.bfloat16),
+            pltpu.VMEM((4, count, WIDE, depth), jnp.bfloat16),
+            pltpu.VMEM((2, 3, 3, 4 * shard, depth), jnp.bfloat16),
+            pltpu.VMEM((tm, 8, LANES), jnp.float32),
+            pltpu.VMEM((tm, flat, LANES), jnp.bfloat16),
+            pltpu.VMEM((tm, flat, LANES), jnp.bfloat16),
+            dma((tm,)),
+            dma((tm,)),
+            dma((tm,)),
+            dma((tm,)),
+            dma((2, 3, 3)),
+            dma((2, 3, 3)),
+            dma((2, 2 * tm)),
+            dma((2, 2 * tm)),
+            dma((tm,)),
+            dma((tm,)),
+            dma((tm,)),
+            dma((tm,)),
+            dma((2, 3)),
+        ],
+        compiler_params=pltpu.CompilerParams(
+            collective_id=0, has_side_effects=True, vmem_limit_bytes=48 * 1024 * 1024
+        ),
+    )(
+        frames.reshape(flat, depth),
+        jnp.transpose(w_in, (0, 1, 3, 2)),
+        jnp.transpose(w_out, (0, 1, 3, 2)),
+        decay_codes.reshape(1, -1),
+        resets,
+    )
+    return out.reshape(frames.shape)
+
+
+def on_device(frames, w_in, w_out, decay_codes, resets):
+    tm, row = (lax.axis_size("tm"), lax.axis_size("row"))
+    own, height, width, depth = frames.shape
+    fits = (
+        row == 4
+        and tm > 1
+        and height == 2
+        and own <= 8
+        and width < WIDE
+        and own * height * width % 16 == 0
+        and 2 * width % 16 == 0
+        and w_in.shape[3] * row == LANES
+        and depth == tm * LANES
+    )
+    plan = by_channels if fits else by_filters
+    return plan(frames, w_in, w_out, decay_codes, resets)
 
 
 def solution(mesh):

time: 141 us -> 39.4 us (0.28)
  waiting for transfers between devices: 58.3 us -> 0 us
  Pallas kernels: 0 us -> 35 us
  matrix products: 24.8 us -> 0 us
  blocking collectives: 23.8 us -> 0 us
  starting transfers between devices: 15.9 us -> 0 us
  between operations: 13.6 us -> 0.01 us
  local copies, waits for them, and re-layouts: 0.97 us -> 4.14 us
  other arithmetic: 2.77 us -> 0 us
    all_gather x2 -> x0, waiting for transfers between devices: 55 us -> none  [the longest x1 45.6 us: on_device(): lax.all_gather(w_in, ('tm', 'row'), axis=3, tiled=True)]
    pallas_call x0 -> x1, Pallas kernels: none -> 35 us  [by_channels(): pl.pallas_call(functools.partial(layer_kernel, tm, width), out_shape=jax....]
    dot_general x18 -> x0, matrix products: 24.8 us -> none  [conv_rows(): jnp.einsum('frwc,ck->frwk', padded[:, i:i + height, j:j + width], weight[...]
    all_gather x2 -> x0, blocking collectives: 23.8 us -> none  [entering(): gathered = jax.tree.map(lambda a: lax.all_gather(a, axis), part)]
    ppermute x4 -> x0, starting transfers between devices: 15.8 us -> none  [the longest x2 12 us: extended_2(): before = lax.ppermute(last, axis, up)]
    unnamed x3 -> x11, local copies, waits for them, and re-layouts: 0.01 us -> 4.14 us
    ppermute x4 -> x0, waiting for transfers between devices: 1.96 us -> none  [the longest x2 1.96 us: extended_2(): after = lax.ppermute(initial, axis, down)]
  transfers between devices with their start and end apart: 6 -> 0, of which waited for: 3 -> 0; matrix products, arithmetic and copies ran while one was open for 12% -> 0% of each run, Pallas kernels for 0% -> 0%
where the time goes in v2:
time: 39.4 us; the launch traced here: 39.2 us
  Pallas kernels  35 us (89%)
  local copies, waits for them, and re-layouts  4.14 us (11%)
    pallas_call x1, Pallas kernels, by_channels(): pl.pallas_call(functools.partial(layer_kernel, tm, width), out_shape=jax....  35 us
    unnamed x11, local copies, waits for them, and re-layouts  4.14 us

profile of v2, /device:TPU:1, one launch (start us, length us, event | category | flops | bytes accessed | tf_op | source)
XLA Modules:
  0.0 39.2 jit_solution(2350115902152746535)
XLA Ops:
  0.0 0.0 copy-start.3
  0.0 0.0 copy-start.4
  0.0 0.7 %copy-done.3 = s32[512]{0:T(512)S(1)} copy-done((s32[512]{0:T(512)S(1)}, s32[512]{0:T(512)}, u32[]{:S(2)}) %copy-start.3) | copy-done | bytes 2072
  0.7 0.0 copy-done.4
  0.7 0.0 copy-start
  0.7 1.0 %copy-done = bf16[3,3,512,32]{2,3,1,0:T(8,128)(2,1)S(1)} copy-done((bf16[3,3,512,32]{2,3,1,0:T(8,128)(2,1)S(1)}, bf16[3,3,512,32]{2,3,1,0:T(8,128)(2,1)}, u32[]{:S(2)}) %copy-start) | copy-done | bytes 294936
  1.6 0.0 copy-start.1
  1.6 1.0 %copy-done.1 = bf16[3,3,512,32]{2,3,1,0:T(8,128)(2,1)S(1)} copy-done((bf16[3,3,512,32]{2,3,1,0:T(8,128)(2,1)S(1)}, bf16[3,3,512,32]{2,3,1,0:T(8,128)(2,1)}, u32[]{:S(2)}) %copy-start.1) | copy-done | bytes 294936
  2.6 0.0 copy-start.2
  2.6 0.9 %copy-done.2 = bf16[2,2,24,512]{3,2,1,0:T(8,128)(2,1)S(1)} copy-done((bf16[2,2,24,512]{3,2,1,0:T(8,128)(2,1)S(1)}, bf16[2,2,24,512]{3,2,1,0:T(8,128)(2,1)}, u32[]{:S(2)}) %copy-start.2) | copy-done | bytes 98328
  3.5 35.0 %shard_map.55 = bf16[96,512]{1,0:T(8,128)(2,1)S(1)} custom-call(bf16[96,512]{1,0:T(8,128)(2,1)S(1)} %bitcast.8, bf16[3,3,32,512]{3,2,1,0:T(8,128)(2,1)S(1)} %bitcast.6, bf16[3,3,32,512]{3,2,1,0:T(8,128)(2,1)S(1)} %bitcast.7, s32[1,512]{1,0:T(1,128)S(1)} %bitcast.9, s32[2]{0:T(128)S(1)} %copy-done.4), custom_call_target="tpu_custom_call" | custom-call | tf_op jit(solution)/shard_map/pallas_call | solution.py:399
  38.5 0.6 %copy.7 = bf16[2,2,24,512]{3,2,1,0:T(8,128)(2,1)} copy(bf16[2,2,24,512]{3,2,1,0:T(8,128)(2,1)S(1)} %bitcast.5) | data formatting | bytes 196608
Async XLA Ops:
  0.0 0.7 %copy-start.3 = (s32[512]{0:T(512)S(1)}, s32[512]{0:T(512)}, u32[]{:S(2)}) copy-start(s32[512]{0:T(512)} %param.8) | copy-start | bytes 6148
  0.0 0.7 %copy-start.4 = (s32[2]{0:T(128)S(1)}, s32[2]{0:T(128)}, u32[]{:S(2)}) copy-start(s32[2]{0:T(128)} %resets_ref.1) | copy-start | bytes 28
  0.7 1.0 %copy-start = (bf16[3,3,512,32]{2,3,1,0:T(8,128)(2,1)S(1)}, bf16[3,3,512,32]{2,3,1,0:T(8,128)(2,1)}, u32[]{:S(2)}) copy-start(bf16[3,3,512,32]{2,3,1,0:T(8,128)(2,1)} %param.6) | copy-start | bytes 884740
  1.6 1.0 %copy-start.1 = (bf16[3,3,512,32]{2,3,1,0:T(8,128)(2,1)S(1)}, bf16[3,3,512,32]{2,3,1,0:T(8,128)(2,1)}, u32[]{:S(2)}) copy-start(bf16[3,3,512,32]{2,3,1,0:T(8,128)(2,1)} %param.7) | copy-start | bytes 884740
  2.6 0.9 %copy-start.2 = (bf16[2,2,24,512]{3,2,1,0:T(8,128)(2,1)S(1)}, bf16[2,2,24,512]{3,2,1,0:T(8,128)(2,1)}, u32[]{:S(2)}) copy-start(bf16[2,2,24,512]{3,2,1,0:T(8,128)(2,1)} %param.5) | copy-start | bytes 294916

commit v3 on v2

--- a/solution.py
+++ b/solution.py
@@ -138,6 +138,7 @@
     o_send,
     o_recv,
     own_sem,
+    codes_in,
 ):
     z, r = (lax.axis_index("tm"), lax.axis_index("row"))
     rows = lax.axis_size("row")
@@ -147,6 +148,10 @@
     own = frames_ref.shape[0] // (2 * width)
     count = own * tm
     depth = frames_ref.shape[1]
+    first = pltpu.make_async_copy(frames_ref, blocks.at[z], own_sem.at[0])
+    first.start()
+    table = pltpu.make_async_copy(codes_ref, codes_in, own_sem.at[1])
+    table.start()
     started = []
     mine_copies = []
 
@@ -185,7 +190,7 @@
                 )
                 copy.start()
                 copies.append(copy)
-            mine = pltpu.make_async_copy(ref.at[i], bank_slot(b, i, r), own_sem.at[b, i])
+            mine = pltpu.make_async_copy(ref.at[i], bank_slot(b, i, r), own_sem.at[2 + 3 * b + i])
             mine.start()
             mine_copies.append(mine)
         started.extend(c.wait_send for c in copies)
@@ -208,8 +213,56 @@
             copies.append((d, copy))
         return copies
 
-    def edge_copies(stage, array, d, part):
-        slot = d + stage * tm
+    def line(origin, slots, send, recv, arrived, between):
+        def hop(way, k):
+            source = z - k if way == 0 else z + k
+            to = z + 1 if way == 0 else z - 1
+            src = origin if k == 0 else slots.at[source]
+            return remote(
+                src, slots.at[source], send.at[way, k], recv.at[way, k], tm=to
+            )
+
+        def sends(way, k):
+            if way == 0:
+                return (z >= k) & (z < tm - 1)
+            return (z + k < tm) & (z > 0)
+
+        def from_there(way, k):
+            return z >= k if way == 0 else z + k < tm
+
+        def when_start(way, k):
+            @pl.when(sends(way, k))
+            def _():
+                hop(way, k).start()
+
+        for way in range(2):
+            when_start(way, 0)
+        yield
+        for k in range(1, tm):
+            for way in range(2):
+                source = z - k if way == 0 else z + k
+
+                @pl.when(from_there(way, k))
+                def _():
+                    remote(
+                        slots.at[source], slots.at[source], send.at[way, k], recv.at[way, k - 1],
+                        tm=source,
+                    ).wait_recv()
+                    if k < tm - 1:
+                        when_start(way, k)
+                    arrived(source)
+
+            between(k - 1)
+        yield
+        for way in range(2):
+            for k in range(tm - 1):
+                @pl.when(sends(way, k))
+                def _():
+                    hop(way, k).wait_send()
+        yield
+
+    def edge_copies(stage, array, source, part):
+        slot = source + stage * tm
         up = remote(
             part(array, 1), part(array, 3), e_send.at[0, slot], e_recv.at[0, slot],
             row=jnp.maximum(r - 1, 0),
@@ -254,9 +307,18 @@
     keeps = spread(
         lambda d, to: remote(keep.at[z], keep.at[z], k_send.at[d], k_recv.at[d], tm=to)
     )
-    arriving = spread(
-        lambda d, to: remote(frames_ref, blocks.at[z], f_send.at[d], f_recv.at[d], tm=to)
-    )
+    relays = []
+
+    def frames_arrived(source):
+        place_frames(blocks.at[source], source)
+        start_edges(edge_copies(0, image, source, frame_part(source)))
+
+    def relay_in(n):
+        if n < 3:
+            relays.append(bank_relay(0, n, in_copies))
+
+    frames_line = line(frames_ref, blocks, f_send, f_recv, frames_arrived, relay_in)
+    next(frames_line)
     in_copies = bank_sends(0, win_ref)
 
     @pl.when(r == 0)
@@ -282,19 +344,10 @@
     def frame_part(source):
         return lambda array, y: array.at[y, pl.ds(source * own, own)]
 
-    place_frames(frames_ref, z)
-    edges = [edge_copies(0, image, 0, frame_part(z))]
-    start_edges(edges[0])
-    relays = []
-    for n, (d, copy) in enumerate(arriving):
-        copy.wait_recv()
-        source = lax.rem(z - d + tm, tm)
-        place_frames(blocks.at[source], source)
-        pair = edge_copies(0, image, d, frame_part(source))
-        start_edges(pair)
-        edges.append(pair)
-        if n < 3:
-            relays.append(bank_relay(0, n, in_copies))
+    first.wait()
+    frames_arrived(z)
+    next(frames_line)
+    edges = [edge_copies(0, image, n, frame_part(n)) for n in range(tm)]
     for n in range(len(relays), 3):
         relays.append(bank_relay(0, n, in_copies))
     out_copies = bank_sends(1, wout_ref)
@@ -322,7 +375,8 @@
         return (left + total[:, LANES : 2 * LANES] + right).reshape(2, count, WIDE, LANES)
 
     drive = conv(image, 0)
-    codes = codes_ref[:, pl.ds(pl.multiple_of(z * LANES, LANES), LANES)].astype(jnp.float32)
+    table.wait()
+    codes = codes_in[:, pl.ds(pl.multiple_of(z * LANES, LANES), LANES)].astype(jnp.float32)
     rates = jnp.exp(
         WINDOW / count * (LOW_LOG + codes / (LEVELS - 1) * (HIGH_LOG - LOW_LOG))
     )
@@ -336,29 +390,31 @@
         hidden_own[t] = value.reshape(2 * width, LANES)
         hidden[1:3, t, :, here] = jnp.concatenate([value, tail], axis=1)
 
-    arriving = spread(
-        lambda d, to: remote(hidden_own, hidden_in.at[z], h_send.at[d], h_recv.at[d], tm=to)
-    )
-
     def lane_part(source):
-        lanes = pl.ds(pl.multiple_of(source * LANES, LANES), LANES)
+        at = source * LANES
+        lanes = pl.ds(at if isinstance(at, int) else pl.multiple_of(at, LANES), LANES)
         return lambda array, y: array.at[y, :, :, lanes]
 
-    second = [edge_copies(1, hidden, 0, lane_part(z))]
-    start_edges(second[0])
     relays = []
-    for n, (d, copy) in enumerate(arriving):
-        if n < 3:
-            relays.append(bank_relay(1, n, out_copies))
-        copy.wait_recv()
-        source = lax.rem(z - d + tm, tm)
+
+    def hidden_arrived(source):
         lanes = pl.ds(pl.multiple_of(source * LANES, LANES), LANES)
         for t in range(count):
             value = hidden_in[source, t].reshape(2, width, LANES)
             hidden[1:3, t, :, lanes] = jnp.concatenate([value, tail], axis=1)
-        pair = edge_copies(1, hidden, d, lane_part(source))
-        start_edges(pair)
-        second.append(pair)
+        start_edges(edge_copies(1, hidden, source, lane_part(source)))
+
+    def relay_out(n):
+        if n < 3:
+            relays.append(bank_relay(1, n, out_copies))
+
+    hidden_line = line(hidden_own, hidden_in, h_send, h_recv, hidden_arrived, relay_out)
+    next(hidden_line)
+    start_edges(edge_copies(1, hidden, z, lane_part(z)))
+    next(hidden_line)
+    second = [
+        edge_copies(1, hidden, n, lambda array, y, n=n: lane_part(n)(array, y)) for n in range(tm)
+    ]
     for n in range(len(relays), 3):
         relays.append(bank_relay(1, n, out_copies))
     for n in range(3):
@@ -384,6 +440,8 @@
         out_ref[:, pl.ds(pl.multiple_of(source * LANES, LANES), LANES)] = result_in[source]
     for wait in started:
         wait()
+    next(frames_line)
+    next(hidden_line)
     finish_edges(edges)
     finish_edges(second)
 
@@ -399,7 +457,7 @@
     out = pl.pallas_call(
         functools.partial(layer_kernel, tm, width),
         out_shape=jax.ShapeDtypeStruct((flat, depth), jnp.bfloat16),
-        in_specs=[vmem] * 4 + [pl.BlockSpec(memory_space=pltpu.SMEM)],
+        in_specs=[pl.BlockSpec(memory_space=pl.ANY)] * 4 + [pl.BlockSpec(memory_space=pltpu.SMEM)],
         out_specs=vmem,
         scratch_shapes=[
             pltpu.VMEM((tm, flat, depth), jnp.bfloat16),
@@ -411,22 +469,23 @@
             pltpu.VMEM((tm, 8, LANES), jnp.float32),
             pltpu.VMEM((tm, flat, LANES), jnp.bfloat16),
             pltpu.VMEM((tm, flat, LANES), jnp.bfloat16),
-            dma((tm,)),
-            dma((tm,)),
+            dma((2, tm)),
+            dma((2, tm)),
             dma((tm,)),
             dma((tm,)),
             dma((2, 3, 3)),
             dma((2, 3, 3)),
             dma((2, 2 * tm)),
             dma((2, 2 * tm)),
+            dma((2, tm)),
+            dma((2, tm)),
             dma((tm,)),
             dma((tm,)),
-            dma((tm,)),
-            dma((tm,)),
-            dma((2, 3)),
+            dma((8,)),
+            pltpu.VMEM((1, depth), jnp.int32),
         ],
         compiler_params=pltpu.CompilerParams(
-            collective_id=0, has_side_effects=True, vmem_limit_bytes=48 * 1024 * 1024
+            collective_id=0, has_side_effects=True, vmem_limit_bytes=60 * 1024 * 1024
         ),
     )(
         frames.reshape(flat, depth),

time: 39.4 us -> 41.2 us (1.046)
  Pallas kernels: 35 us -> 39.5 us
  local copies, waits for them, and re-layouts: 4.14 us -> 1.54 us
    pallas_call x1, Pallas kernels: 35 us -> 39.5 us  [by_channels(): pl.pallas_call(functools.partial(layer_kernel, tm, width), out_shape=jax....]
    unnamed x11 -> x1, local copies, waits for them, and re-layouts: 4.14 us -> 1.54 us
where the time goes in v3:
time: 41.2 us; the launch traced here: 41.1 us
  Pallas kernels  39.5 us (96%)
  local copies, waits for them, and re-layouts  1.54 us (4%)
    pallas_call x1, Pallas kernels, by_channels(): pl.pallas_call(functools.partial(layer_kernel, tm, width), out_shape=jax....  39.5 us
    unnamed x1, local copies, waits for them, and re-layouts  1.54 us

profile of v3, /device:TPU:1, one launch (start us, length us, event | category | flops | bytes accessed | tf_op | source)
XLA Modules:
  0.0 41.1 jit_solution(10881587792706155188)
XLA Ops:
  0.0 39.5 %shard_map.55 = bf16[96,512]{1,0:T(8,128)(2,1)} custom-call(bf16[96,512]{1,0:T(8,128)(2,1)} %bitcast.8, bf16[3,3,32,512]{3,2,1,0:T(8,128)(2,1)} %bitcast.6, bf16[3,3,32,512]{3,2,1,0:T(8,128)(2,1)} %bitcast.7, s32[1,512]{1,0:T(1,128)} %bitcast.9, s32[2]{0:T(128)} %resets_ref.1), custom_call_target="tpu_custom_call" | custom-call | tf_op jit(solution)/shard_map/pallas_call | solution.py:457
  39.6 1.5 %copy.7 = bf16[2,2,24,512]{3,2,1,0:T(8,128)(2,1)} copy(bf16[2,2,24,512]{3,2,1,0:T(8,128)(2,1)} %bitcast.5) | data formatting | bytes 196608

commit v4 on v2

--- a/solution.py
+++ b/solution.py
@@ -138,6 +138,7 @@
     o_send,
     o_recv,
     own_sem,
+    codes_in,
 ):
     z, r = (lax.axis_index("tm"), lax.axis_index("row"))
     rows = lax.axis_size("row")
@@ -147,6 +148,10 @@
     own = frames_ref.shape[0] // (2 * width)
     count = own * tm
     depth = frames_ref.shape[1]
+    first = pltpu.make_async_copy(frames_ref, blocks.at[z], own_sem.at[0])
+    first.start()
+    table = pltpu.make_async_copy(codes_ref, codes_in, own_sem.at[1])
+    table.start()
     started = []
     mine_copies = []
 
@@ -185,7 +190,7 @@
                 )
                 copy.start()
                 copies.append(copy)
-            mine = pltpu.make_async_copy(ref.at[i], bank_slot(b, i, r), own_sem.at[b, i])
+            mine = pltpu.make_async_copy(ref.at[i], bank_slot(b, i, r), own_sem.at[2 + 3 * b + i])
             mine.start()
             mine_copies.append(mine)
         started.extend(c.wait_send for c in copies)
@@ -282,7 +287,8 @@
     def frame_part(source):
         return lambda array, y: array.at[y, pl.ds(source * own, own)]
 
-    place_frames(frames_ref, z)
+    first.wait()
+    place_frames(blocks.at[z], z)
     edges = [edge_copies(0, image, 0, frame_part(z))]
     start_edges(edges[0])
     relays = []
@@ -304,25 +310,31 @@
         in_copies[2 * n + 1].wait_recv()
         relays[n].wait_recv()
         mine_copies[n].wait()
-    wait_edges(edges)
-
-    def conv(array, b):
-        total = None
-        for i in range(3):
-            term = lax.dot_general(
-                array[i : i + 2].reshape(2 * count * WIDE, depth),
-                banks[b, i].reshape(3 * LANES, depth),
-                (((1,), (1,)), ((), ())),
-                preferred_element_type=jnp.float32,
-            )
-            total = term if total is None else total + term
+
+    def taps(rows, b, i):
+        return lax.dot_general(
+            rows.reshape(-1, depth),
+            banks[b, i].reshape(3 * LANES, depth),
+            (((1,), (1,)), ((), ())),
+            preferred_element_type=jnp.float32,
+        )
+
+    def conv(array, b, pairs):
+        inner = taps(array[1:3], b, 1)
+        top = taps(array[2], b, 2)
+        bottom = taps(array[1], b, 0)
+        wait_edges(pairs)
+        top = top + taps(array[0], b, 0)
+        bottom = bottom + taps(array[3], b, 2)
+        total = inner + jnp.concatenate([top, bottom], axis=0)
         size = 2 * count * WIDE
         left = pltpu.roll(total[:, :LANES], 1, 0)
         right = pltpu.roll(total[:, 2 * LANES :], size - 1, 0)
         return (left + total[:, LANES : 2 * LANES] + right).reshape(2, count, WIDE, LANES)
 
-    drive = conv(image, 0)
-    codes = codes_ref[:, pl.ds(pl.multiple_of(z * LANES, LANES), LANES)].astype(jnp.float32)
+    drive = conv(image, 0, edges)
+    table.wait()
+    codes = codes_in[:, pl.ds(pl.multiple_of(z * LANES, LANES), LANES)].astype(jnp.float32)
     rates = jnp.exp(
         WINDOW / count * (LOW_LOG + codes / (LEVELS - 1) * (HIGH_LOG - LOW_LOG))
     )
@@ -364,10 +376,9 @@
     for n in range(3):
         out_copies[2 * n + 1].wait_recv()
         relays[n].wait_recv()
-    wait_edges(second)
     for n in range(3, 6):
         mine_copies[n].wait()
-    mixed = conv(hidden, 1).astype(jnp.bfloat16)
+    mixed = conv(hidden, 1, second).astype(jnp.bfloat16)
     for k in range(tm):
         result_out[k] = jnp.concatenate(
             [mixed[y, k * own + f, :width] for f in range(own) for y in range(2)], axis=0
@@ -399,7 +410,7 @@
     out = pl.pallas_call(
         functools.partial(layer_kernel, tm, width),
         out_shape=jax.ShapeDtypeStruct((flat, depth), jnp.bfloat16),
-        in_specs=[vmem] * 4 + [pl.BlockSpec(memory_space=pltpu.SMEM)],
+        in_specs=[pl.BlockSpec(memory_space=pl.ANY)] * 4 + [pl.BlockSpec(memory_space=pltpu.SMEM)],
         out_specs=vmem,
         scratch_shapes=[
             pltpu.VMEM((tm, flat, depth), jnp.bfloat16),
@@ -423,10 +434,11 @@
             dma((tm,)),
             dma((tm,)),
             dma((tm,)),
-            dma((2, 3)),
+            dma((8,)),
+            pltpu.VMEM((1, depth), jnp.int32),
         ],
         compiler_params=pltpu.CompilerParams(
-            collective_id=0, has_side_effects=True, vmem_limit_bytes=48 * 1024 * 1024
+            collective_id=0, has_side_effects=True, vmem_limit_bytes=60 * 1024 * 1024
         ),
     )(
         frames.reshape(flat, depth),

time: 39.4 us -> 38 us (0.964)
  local copies, waits for them, and re-layouts: 4.14 us -> 1.54 us
  Pallas kernels: 35 us -> 36.3 us
    unnamed x11 -> x1, local copies, waits for them, and re-layouts: 4.14 us -> 1.54 us
    pallas_call x1, Pallas kernels: 35 us -> 36.3 us  [by_channels(): pl.pallas_call(functools.partial(layer_kernel, tm, width), out_shape=jax....]
where the time goes in v4:
time: 38 us; the launch traced here: 37.9 us
  Pallas kernels  36.3 us (96%)
  local copies, waits for them, and re-layouts  1.54 us (4%)
    pallas_call x1, Pallas kernels, by_channels(): pl.pallas_call(functools.partial(layer_kernel, tm, width), out_shape=jax....  36.3 us
    unnamed x1, local copies, waits for them, and re-layouts  1.54 us

profile of v4, /device:TPU:1, one launch (start us, length us, event | category | flops | bytes accessed | tf_op | source)
XLA Modules:
  0.0 37.9 jit_solution(17516802011471560464)
XLA Ops:
  0.0 36.3 %shard_map.55 = bf16[96,512]{1,0:T(8,128)(2,1)} custom-call(bf16[96,512]{1,0:T(8,128)(2,1)} %bitcast.8, bf16[3,3,32,512]{3,2,1,0:T(8,128)(2,1)} %bitcast.6, bf16[3,3,32,512]{3,2,1,0:T(8,128)(2,1)} %bitcast.7, s32[1,512]{1,0:T(1,128)} %bitcast.9, s32[2]{0:T(128)} %resets_ref.1), custom_call_target="tpu_custom_call" | custom-call | tf_op jit(solution)/shard_map/pallas_call | solution.py:410
  36.3 1.5 %copy.7 = bf16[2,2,24,512]{3,2,1,0:T(8,128)(2,1)} copy(bf16[2,2,24,512]{3,2,1,0:T(8,128)(2,1)} %bitcast.5) | data formatting | bytes 196608

commit v5 on v4

--- a/solution.py
+++ b/solution.py
@@ -341,36 +341,47 @@
     state = jnp.zeros((2, width, LANES), jnp.float32)
     tail = jnp.zeros((2, WIDE - width, LANES), jnp.bfloat16)
     here = pl.ds(pl.multiple_of(z * LANES, LANES), LANES)
+    piece = count // 2
+    arriving, second = ([], [])
+
+    def hidden_copy(part, d, to):
+        frames_of = pl.ds(part * piece, piece)
+        return remote(
+            hidden_own.at[frames_of], hidden_in.at[z, frames_of],
+            h_send.at[d + part * tm], h_recv.at[d + part * tm], tm=to,
+        )
+
+    def lane_part(source, part):
+        lanes = pl.ds(pl.multiple_of(source * LANES, LANES), LANES)
+        return lambda array, y: array.at[y, pl.ds(part * piece, piece), :, lanes]
+
     for t in range(count):
         gate = keep[t // own, t % own : t % own + 1, :] * rates
         state = gate[None] * state + drive[:, t, :width]
         value = jax.nn.gelu(state).astype(jnp.bfloat16)
         hidden_own[t] = value.reshape(2 * width, LANES)
         hidden[1:3, t, :, here] = jnp.concatenate([value, tail], axis=1)
-
-    arriving = spread(
-        lambda d, to: remote(hidden_own, hidden_in.at[z], h_send.at[d], h_recv.at[d], tm=to)
-    )
-
-    def lane_part(source):
-        lanes = pl.ds(pl.multiple_of(source * LANES, LANES), LANES)
-        return lambda array, y: array.at[y, :, :, lanes]
-
-    second = [edge_copies(1, hidden, 0, lane_part(z))]
-    start_edges(second[0])
+        if (t + 1) % piece == 0:
+            part = t // piece
+            arriving.append(spread(functools.partial(hidden_copy, part)))
+            pair = edge_copies(1 + part, hidden, 0, lane_part(z, part))
+            start_edges(pair)
+            second.append(pair)
+
     relays = []
-    for n, (d, copy) in enumerate(arriving):
-        if n < 3:
-            relays.append(bank_relay(1, n, out_copies))
-        copy.wait_recv()
-        source = lax.rem(z - d + tm, tm)
-        lanes = pl.ds(pl.multiple_of(source * LANES, LANES), LANES)
-        for t in range(count):
-            value = hidden_in[source, t].reshape(2, width, LANES)
-            hidden[1:3, t, :, lanes] = jnp.concatenate([value, tail], axis=1)
-        pair = edge_copies(1, hidden, d, lane_part(source))
-        start_edges(pair)
-        second.append(pair)
+    for part in range(2):
+        for d, copy in arriving[part]:
+            if len(relays) < 3:
+                relays.append(bank_relay(1, len(relays), out_copies))
+            copy.wait_recv()
+            source = lax.rem(z - d + tm, tm)
+            lanes = pl.ds(pl.multiple_of(source * LANES, LANES), LANES)
+            for t in range(part * piece, (part + 1) * piece):
+                value = hidden_in[source, t].reshape(2, width, LANES)
+                hidden[1:3, t, :, lanes] = jnp.concatenate([value, tail], axis=1)
+            pair = edge_copies(1 + part, hidden, d, lane_part(source, part))
+            start_edges(pair)
+            second.append(pair)
     for n in range(len(relays), 3):
         relays.append(bank_relay(1, n, out_copies))
     for n in range(3):
@@ -428,10 +439,10 @@
             dma((tm,)),
             dma((2, 3, 3)),
             dma((2, 3, 3)),
-            dma((2, 2 * tm)),
-            dma((2, 2 * tm)),
-            dma((tm,)),
-            dma((tm,)),
+            dma((2, 3 * tm)),
+            dma((2, 3 * tm)),
+            dma((2 * tm,)),
+            dma((2 * tm,)),
             dma((tm,)),
             dma((tm,)),
             dma((8,)),
@@ -458,6 +469,7 @@
         and tm > 1
         and height == 2
         and own <= 8
+        and own * tm % 2 == 0
         and width < WIDE
         and own * height * width % 16 == 0
         and 2 * width % 16 == 0

time: 38 us -> 37.6 us (0.989)
  Pallas kernels: 36.3 us -> 35.9 us
    pallas_call x1, Pallas kernels: 36.3 us -> 35.9 us  [by_channels(): pl.pallas_call(functools.partial(layer_kernel, tm, width), out_shape=jax....]
where the time goes in v5:
time: 37.6 us; the launch traced here: 37.5 us
  Pallas kernels  35.9 us (95%)
  local copies, waits for them, and re-layouts  1.54 us (4%)
    pallas_call x1, Pallas kernels, by_channels(): pl.pallas_call(functools.partial(layer_kernel, tm, width), out_shape=jax....  35.9 us
    unnamed x1, local copies, waits for them, and re-layouts  1.54 us

profile of v5, /device:TPU:1, one launch (start us, length us, event | category | flops | bytes accessed | tf_op | source)
XLA Modules:
  0.0 37.5 jit_solution(15932173678328499791)
XLA Ops:
  0.0 35.9 %shard_map.55 = bf16[96,512]{1,0:T(8,128)(2,1)} custom-call(bf16[96,512]{1,0:T(8,128)(2,1)} %bitcast.8, bf16[3,3,32,512]{3,2,1,0:T(8,128)(2,1)} %bitcast.6, bf16[3,3,32,512]{3,2,1,0:T(8,128)(2,1)} %bitcast.7, s32[1,512]{1,0:T(1,128)} %bitcast.9, s32[2]{0:T(128)} %resets_ref.1), custom_call_target="tpu_custom_call" | custom-call | tf_op jit(solution)/shard_map/pallas_call | solution.py:421
  35.9 1.5 %copy.7 = bf16[2,2,24,512]{3,2,1,0:T(8,128)(2,1)} copy(bf16[2,2,24,512]{3,2,1,0:T(8,128)(2,1)} %bitcast.5) | data formatting | bytes 196608
